TPU v7x, 512 devices: a whole 4x8x8 slice. The times are simulated.
512 devices in a mesh: dp: 32 (over x, z), seq: 16 (over y, core).
Axes of the slice: x: 4, y: 8, z: 8, core: 2. Of those that a mesh axis runs over, the one named last changes fastest.
Arguments:
- projected: bfloat16 [32, 2048, 3, 1536], P('dp', 'seq'), may hold values from -6 to 6
- cotangent: bfloat16 [32, 2048, 1152], P('dp', 'seq'), may hold values from -6 to 6
- out_weight: bfloat16 [1536, 1152], P('seq'), may hold values from -0.15625 to 0.15625
- norm_gain: float32 [1536], replicated, may hold values from 0.1 to 1.9
- conv_taps: float32 [9, 1536], replicated, may hold values from -2.5 to 2.5
- feature_seeds: int32 [48], replicated, may hold values from 0 to 1073741823
- packing: int32 [32, 5, 2048], P('dp', None, 'seq'), may hold values from 0 to 68, as said below
Outputs:
- block_out: bfloat16 [32, 2048, 1152], P('dp', 'seq')
- grad_projected: bfloat16 [32, 2048, 3, 1536], P('dp', 'seq')
- grad_out_weight: float32 [1536, 1152], P('seq')
- grad_norm_gain: float32 [1536], replicated
- grad_conv_taps: float32 [9, 1536], replicated
Inputs may be any that keep to these rules, and one draw needn't show every extreme that they name: `packing`: in each pack, images 0 to 2 follow one another, each contiguous and row-major; rows 1 and 2 give a token's row and column in its image, rows 3 and 4 the image's width and height. Widths are multiples of 16 up to 64; image 1 of every pack is 64 wide and directly precedes the last image; the last image of every pack is 16 wide and holds the pack's last 1088 tokens; heights are at least 2; every pack holds 3 images and no padding.
All inputs are finite; a program needn't handle non-finite values.
Results may differ from a plain program's by a relative error of at most 0.012.
Values may be sent and summed in bfloat16 or wider, within the bound.
No kernel may reach another device: no remote copies, remote signals or barrier semaphores. Data moves between devices by JAX's collectives and lax.ppermute only.
A program may use at most 128 MiB of HBM per device.

v0:
```python
import math
import jax
import jax.numpy as jnp
from jax import lax
from jax.sharding import PartitionSpec as P

HEAD = 32
FEAT = 256
IMGS = 3
WMAX = 64
feature_floor = 0.1
epsilon = 1e-06
highest = lax.Precision.HIGHEST


def with_halo(shard, sides, width):
    for axis, dim in sides:
        devices, length = (lax.axis_size(axis), shard.shape[dim])
        up = [(i, (i + 1) % devices) for i in range(devices - 1)]
        down = [(j, i) for i, j in up]
        last = lax.slice_in_dim(shard, length - width, length, axis=dim)
        initial = lax.slice_in_dim(shard, 0, width, axis=dim)
        before = lax.ppermute(last, axis, up)
        after = lax.ppermute(initial, axis, down)
        shard = jnp.concatenate([before, shard, after], axis=dim)
    return shard


def feature_matrix(seed_list):
    counter = jnp.arange(HEAD * FEAT, dtype=jnp.int32).reshape(1, HEAD, FEAT)
    hashed = seed_list[:, None, None] * -1640531535 + counter
    hashed = hashed ^ hashed >> 16 & 65535
    hashed = hashed * -2048144789
    hashed = hashed ^ hashed >> 13 & 524287
    hashed = hashed * -1028477387
    hashed = hashed ^ hashed >> 16 & 65535
    top_bits = hashed >> 8 & 16777215
    uniform = top_bits.astype(jnp.float32) * (1.0 / 16777216.0)
    return (1.7320508 * (2.0 * uniform - 1.0)).astype(jnp.bfloat16)


def neighbour(padded, margin, packing_rows, tap_index, direction):
    row_count = packing_rows.shape[1]
    step_row = tap_index // 3 - 1
    step_col = tap_index % 3 - 1
    position = jnp.arange(row_count, dtype=jnp.int32)
    row_width = packing_rows[3]
    new_row = packing_rows[1] + direction * step_row
    new_col = packing_rows[2] + direction * step_col
    inside = (new_row >= 0) & (new_row < packing_rows[4]) & (new_col >= 0) & (new_col < row_width)
    source = position + margin + direction * (step_row * row_width + step_col)
    return jnp.where(inside[:, None], jnp.take(padded, source, axis=0), jnp.zeros((), padded.dtype))


def depthwise(padded, margin, packing_rows, tap_table, direction):
    running = jnp.zeros((packing_rows.shape[1], padded.shape[1]), jnp.float32)
    for tap_index in range(9):
        running = running + tap_table[tap_index][None, :] * neighbour(
            padded, margin, packing_rows, tap_index, direction
        ).astype(jnp.float32)
    return running


def tap_grads(grad_conv, padded, margin, packing_rows):
    grad_float = grad_conv.astype(jnp.float32)
    return jnp.stack(
        [
            jnp.sum(
                grad_float
                * neighbour(padded, margin, packing_rows, tap_index, 1).astype(jnp.float32),
                axis=0,
            )
            for tap_index in range(9)
        ]
    )


def heads_last(rows_matrix, head_count):
    return rows_matrix.reshape(rows_matrix.shape[0], head_count, HEAD).transpose(1, 2, 0)


def rows_first(head_matrix):
    return head_matrix.transpose(2, 0, 1).reshape(
        head_matrix.shape[2], head_matrix.shape[0] * head_matrix.shape[1]
    )


def local(projected, cotangent, out_weight, norm_gain, conv_taps, feature_seeds, packing):
    groups = lax.axis_size("seq")
    member = lax.axis_index("seq")
    pack_count = lax.axis_size("dp")
    tokens_in = projected[0]
    grad_in = cotangent[0]
    rows_local = packing[0]
    tok_rows = tokens_in.shape[0]
    width_all = tokens_in.shape[2]
    local_width = width_all // groups
    head_count = local_width // HEAD
    all_rows = tok_rows * groups
    margin = WMAX + 1
    feature_scale = 1.0 / math.sqrt(HEAD)
    rows_all = lax.all_gather(rows_local, "seq", axis=1, tiled=True)
    padded_values = with_halo(tokens_in[:, 2], (("seq", 0),), margin)
    conv_tokens = depthwise(padded_values, margin, rows_local, conv_taps, 1).astype(jnp.bfloat16)
    outgoing = jnp.stack([tokens_in[:, 0], tokens_in[:, 1], conv_tokens], axis=1)
    arrived = lax.all_to_all(
        outgoing.reshape(tok_rows, 3, groups, local_width),
        "seq",
        split_axis=2,
        concat_axis=0,
        tiled=True,
    )
    arrived = arrived.reshape(all_rows, 3, local_width)
    conv_heads = arrived[:, 2]
    omegas = feature_matrix(
        lax.dynamic_slice_in_dim(feature_seeds, member * head_count, head_count, 0)
    )
    queries = heads_last(arrived[:, 0], head_count)
    keys_in = heads_last(arrived[:, 1], head_count)
    values_c = heads_last(conv_heads, head_count)
    onehot_float = (jnp.arange(IMGS, dtype=jnp.int32)[:, None] == rows_all[0][None, :]).astype(
        jnp.float32
    )
    onehot_half = onehot_float.astype(jnp.bfloat16)
    pre_query = (
        jnp.einsum("het,hef->hft", queries, omegas, preferred_element_type=jnp.float32)
        * feature_scale
    )
    pre_key = (
        jnp.einsum("het,hef->hft", keys_in, omegas, preferred_element_type=jnp.float32)
        * feature_scale
    )
    feat_query = (jax.nn.relu(pre_query) + feature_floor).astype(jnp.bfloat16)
    feat_key = (jax.nn.relu(pre_key) + feature_floor).astype(jnp.bfloat16)
    masked_values = onehot_half[None, :, None, :] * values_c[:, None]
    states = jnp.einsum(
        "hft,hiet->hife", feat_key, masked_values, preferred_element_type=jnp.float32
    ).astype(jnp.bfloat16)
    totals = jnp.einsum(
        "hft,it->hif", feat_key, onehot_half, preferred_element_type=jnp.float32
    ).astype(jnp.bfloat16)
    numerator = jnp.sum(
        jnp.einsum("hft,hife->hiet", feat_query, states, preferred_element_type=jnp.float32)
        * onehot_float[None, :, None, :],
        axis=1,
    )
    denominator = jnp.sum(
        jnp.einsum("hft,hif->hit", feat_query, totals, preferred_element_type=jnp.float32)
        * onehot_float[None],
        axis=1,
    )
    attention_heads = rows_first(
        (numerator / denominator[:, None, :]).astype(jnp.bfloat16)
    ).reshape(all_rows, 1, local_width)
    attention = lax.all_to_all(
        attention_heads, "seq", split_axis=0, concat_axis=1, tiled=True
    ).reshape(tok_rows, width_all)
    attn_float = attention.astype(jnp.float32)
    inv_rms = lax.rsqrt(jnp.mean(attn_float * attn_float, axis=1) + epsilon)
    normed = (attn_float * norm_gain[None, :] * inv_rms[:, None]).astype(jnp.bfloat16)
    weight_all = lax.all_gather(out_weight, "seq", axis=0, tiled=True)
    block_sum = jnp.dot(normed, weight_all, preferred_element_type=jnp.float32)
    grad_normed = jnp.einsum("td,ad->ta", grad_in, weight_all, preferred_element_type=jnp.float32)
    pack_gain = jnp.sum(grad_normed * attn_float * inv_rms[:, None], axis=0)
    inner_sum = jnp.sum(norm_gain[None, :] * grad_normed * attn_float, axis=1)
    grad_attention = (
        inv_rms[:, None] * norm_gain[None, :] * grad_normed
        - attn_float * (inv_rms**3 * inner_sum / width_all)[:, None]
    ).astype(jnp.bfloat16)
    grad_arrived, normed_heads = (
        lax.all_to_all(
            grad_attention.reshape(tok_rows, groups, local_width),
            "seq",
            split_axis=1,
            concat_axis=0,
            tiled=True,
        ),
        lax.all_to_all(
            normed.reshape(tok_rows, groups, local_width),
            "seq",
            split_axis=1,
            concat_axis=0,
            tiled=True,
        ),
    )
    normed_rows = normed_heads.reshape(all_rows, local_width)
    weight_local = jnp.einsum(
        "tc,td->cd",
        normed_rows,
        lax.all_gather(grad_in, "seq", axis=0, tiled=True),
        preferred_element_type=jnp.float32,
    )
    weight_sum = lax.psum(weight_local, "dp") / pack_count
    grad_float = heads_last(grad_arrived.reshape(all_rows, local_width), head_count).astype(
        jnp.float32
    )
    grad_numer = (grad_float / denominator[:, None, :]).astype(jnp.bfloat16)
    grad_denom = -jnp.sum(grad_float * numerator, axis=1) / (denominator * denominator)
    masked_grad = onehot_half[None, :, None, :] * grad_numer[:, None]
    weighted = onehot_float[None, :, :] * grad_denom[:, None, :]
    grad_states = jnp.einsum(
        "hft,hiet->hife", feat_query, masked_grad, preferred_element_type=jnp.float32
    ).astype(jnp.bfloat16)
    grad_totals = jnp.einsum(
        "hft,hit->hif", feat_query.astype(jnp.float32), weighted, precision=highest
    ).astype(jnp.bfloat16)
    grad_fq = jnp.einsum("hiet,hife->hft", masked_grad, states, preferred_element_type=jnp.float32)
    grad_fq = grad_fq + jnp.einsum(
        "hit,hif->hft", weighted, totals.astype(jnp.float32), precision=highest
    )
    gate_query = jnp.where(pre_query > 0, grad_fq, 0.0).astype(jnp.bfloat16)
    grad_queries = (
        jnp.einsum("hft,hef->het", gate_query, omegas, preferred_element_type=jnp.float32)
        * feature_scale
    ).astype(jnp.bfloat16)
    grad_fk = jnp.einsum(
        "hiet,hife->hft", masked_values, grad_states, preferred_element_type=jnp.float32
    )
    grad_fk = grad_fk + jnp.einsum(
        "it,hif->hft", onehot_float, grad_totals.astype(jnp.float32), precision=highest
    )
    gate_key = jnp.where(pre_key > 0, grad_fk, 0.0).astype(jnp.bfloat16)
    grad_keys = (
        jnp.einsum("hft,hef->het", gate_key, omegas, preferred_element_type=jnp.float32)
        * feature_scale
    ).astype(jnp.bfloat16)
    grad_conv = jnp.sum(
        jnp.einsum("hft,hife->hiet", feat_key, grad_states, preferred_element_type=jnp.float32)
        * onehot_float[None, :, None, :],
        axis=1,
    )
    grad_conv = rows_first(grad_conv.astype(jnp.bfloat16))
    grad_queries = rows_first(grad_queries)
    grad_keys = rows_first(grad_keys)
    returned = lax.all_to_all(
        jnp.stack([grad_queries, grad_keys, grad_conv], axis=1).reshape(
            all_rows, 3, 1, local_width
        ),
        "seq",
        split_axis=0,
        concat_axis=2,
        tiled=True,
    )
    returned = returned.reshape(tok_rows, 3, width_all)
    conv_grad_tokens = returned[:, 2]
    padded_grads = with_halo(conv_grad_tokens, (("seq", 0),), margin)
    grad_values = depthwise(padded_grads, margin, rows_local, conv_taps, -1).astype(jnp.bfloat16)
    taps_grad = tap_grads(conv_grad_tokens, padded_values, margin, rows_local)
    grad_tokens = jnp.stack([returned[:, 0], returned[:, 1], grad_values], axis=1)
    gain_sum, taps_sum = lax.psum((pack_gain, taps_grad), ("dp", "seq"))
    return (
        block_sum.astype(jnp.bfloat16)[None],
        grad_tokens[None],
        weight_sum,
        gain_sum / pack_count,
        taps_sum / pack_count,
    )


def solution(mesh):
    in_specs = (
        P("dp", "seq", None, None),
        P("dp", "seq", None),
        P("seq", None),
        P(),
        P(),
        P(),
        P("dp", None, "seq"),
    )
    out_specs = (P("dp", "seq", None), P("dp", "seq", None, None), P("seq", None), P(), P())
    return jax.shard_map(local, mesh=mesh, in_specs=in_specs, out_specs=out_specs, check_vma=False)
```

profile of v0, /device:TPU:1, one launch (start us, length us, event | category | flops | bytes accessed | tf_op | source)
XLA Modules:
  0.0 517.5 jit_solution(8278285979322742595)
XLA Ops:
  9.0 8.8 %collective-permute-start.1 = (bf16[65,1536]{1,0:T(8,128)(2,1)S(1)}, bf16[65,1536]{1,0:T(8,128)(2,1)S(1)}, u32[]{:S(2)}, u32[]{:S(2)}) collective-permute-start(bf16[65,1536]{1,0:T(8,128)(2,1)S(1)} %get-tuple-element.93), channel_id=1, source_target_pairs={{1,0},{2,1},{3,2},{4,3},{5,4},{6,5},{7,6},{8,7},{9,8},{10,9},{11,1... | collective-permute-start | bytes 599048 | tf_op jit(solution)/shard_map/ppermute | solution.py:24
  35.3 3.3 fusion.69
  41.0 4.0 all-to-all-start
  45.8 44.2 %all-gather = s32[1,5,2048]{2,0,1:T(1,128)S(1)} all-gather(s32[1,5,128]{2,0,1:T(1,128)S(1)} %copy-done.60), channel_id=2, replica_groups=mesh['dp'=32,'seq'=16] {'seq'}, dimensions={2}, use_global_device_ids=true | all-gather | bytes 43520 | tf_op jit(solution)/shard_map/all_gather | solution.py:102
  91.3 2.5 fusion.32
  93.8 4.5 add_convert_fusion
  108.0 19.7 %all_to_all.63 = bf16[16,2,6144]{2,1,0:T(2,128)(2,1)} all-to-all(bf16[16,2,6144]{2,1,0:T(2,128)(2,1)S(1)} %reshape.592), channel_id=1, replica_groups=mesh['dp'=32,'seq'=16] {'seq'}, dimensions={0} | all-to-all | bytes 786432 | tf_op jit(solution)/shard_map/all_to_all | solution.py:155
  127.7 3.6 reshape.593
  131.3 2.3 copy.149
  135.9 2.3 copy.151
  138.3 4.3 multiply_reduce_fusion
  144.5 4.6 all-to-all-start.2
  151.2 5.1 fusion.31
  157.4 6.1 %all-to-all-done.2 = bf16[128,16,96]{0,2,1:T(8,128)(2,1)S(1)} async-done(((bf16[128,16,96]{0,2,1:T(8,128)(2,1)}), bf16[128,16,96]{0,2,1:T(8,128)(2,1)S(1)}, u32[]{:S(2)}, u32[]{:S(2)}) %all-to-all-start.2) | async-done | bytes 393248 | tf_op jit(solution)/shard_map/all_to_all | solution.py:171
  164.3 4.1 all-to-all-start.4
  170.9 2.2 reshape.368
  174.6 2.5 convolution_convert_fusion.1
  178.3 3.7 fusion.121
  182.1 4.5 fusion.107
  186.7 4.8 fusion.20
  191.5 4.7 fusion.21
  196.3 4.0 fusion.33
  200.4 2.5 copy.156
  203.0 6.3 %all-to-all-start.3 = ((bf16[2048,3,1,96]{3,1,2,0:T(4,128)(2,1)}), bf16[2048,3,1,96]{3,1,2,0:T(4,128)(2,1)}, u32[]{:S(2)}, u32[]{:S(2)}) async-start(bf16[2048,3,1,96]{3,1,2,0:T(4,128)(2,1)} %copy.156), calls=%async_computation.3 | async-start | bytes 4194304 | tf_op jit(solution)/shard_map/all_to_all | solution.py:235
  211.5 4.3 fusion.4
  218.3 2.6 fusion.22
  220.9 150.5 %all-reduce.3.cloned.1.call-done = f32[96,1152]{1,0:T(8,128)} async-done(((f32[96,1152]{1,0:T(8,128)}), f32[96,1152]{1,0:T(8,128)}) %all-reduce.3.cloned.1.call-update) | async-done | bytes 442384 | tf_op jit(solution)/shard_map/psum | solution.py:193
  373.2 2.9 copy.173
  384.8 7.0 %collective-permute-start.3 = (bf16[65,1536]{1,0:T(8,128)(2,1)S(1)}, bf16[65,1536]{1,0:T(8,128)(2,1)S(1)}, u32[]{:S(2)}, u32[]{:S(2)}) collective-permute-start(bf16[65,1536]{1,0:T(8,128)(2,1)S(1)} %bitcast.347), channel_id=1, source_target_pairs={{1,0},{2,1},{3,2},{4,3},{5,4},{6,5},{7,6},{8,7},{9,8},{10,9},{11,1... | collective-permute-start | bytes 599048 | tf_op jit(solution)/shard_map/ppermute | solution.py:24
  392.1 3.0 collective-permute-start.2
  395.3 96.1 %all-reduce = (f32[1536]{0:T(1024)S(1)}, f32[9,1536]{1,0:T(8,128)S(1)}) all-reduce(f32[1536]{0:T(1024)S(1)} %copy-done.58, f32[9,1536]{1,0:T(8,128)S(1)} %stack.64), channel_id=1, replica_groups=mesh['dp'=32,'seq'=16] {'dp','seq'}, use_global_device_ids=true, to_apply=%region_9.11 | all-reduce | flops 15360 | bytes 122880 | tf_op jit(solution)/shard_map/psum | solution.py:250
  506.2 2.8 fusion.103
  (371 shorter events, 77.4 us)
Async XLA Ops:
  7.2 14.9 %copy-start.60 = (s32[1,5,128]{2,0,1:T(1,128)S(1)}, s32[1,5,128]{2,0,1:T(1,128)}, u32[]{:S(2)}) copy-start(s32[1,5,128]{2,0,1:T(1,128)} %param.15) | copy-start | bytes 7684
  7.2 17.0 %copy-start.59 = (f32[9,1536]{1,0:T(8,128)S(1)}, f32[9,1536]{1,0:T(8,128)}, u32[]{:S(2)}) copy-start(f32[9,1536]{1,0:T(8,128)} %param.13) | copy-start | bytes 165892
  7.2 131.1 %all-gather.5.cloned.1.call-start = ((), (), s32[]{:S(2)}) async-start(), calls=%async_computation.5 | async-start | bytes 3760128 | tf_op jit(solution)/shard_map/all_gather | solution.py:161
  9.0 15.4 %collective-permute-start.1 = (bf16[65,1536]{1,0:T(8,128)(2,1)S(1)}, bf16[65,1536]{1,0:T(8,128)(2,1)S(1)}, u32[]{:S(2)}, u32[]{:S(2)}) collective-permute-start(bf16[65,1536]{1,0:T(8,128)(2,1)S(1)} %get-tuple-element.93), channel_id=1, source_target_pairs={{1,0},{2,1},{3,2},{4,3},{5,4},{6,5},{7,6},{8,7},{9,8},{10,9},{11,1... | collective-permute-start | bytes 599048 | tf_op jit(solution)/shard_map/ppermute | solution.py:24
  17.8 6.6 %collective-permute-start = (bf16[65,1536]{1,0:T(8,128)(2,1)S(1)}, bf16[65,1536]{1,0:T(8,128)(2,1)S(1)}, u32[]{:S(2)}, u32[]{:S(2)}) collective-permute-start(bf16[65,1536]{1,0:T(8,128)(2,1)S(1)} %get-tuple-element.92), channel_id=1, source_target_pairs={{0,1},{1,2},{2,3},{3,4},{4,5},{5,6},{6,7},{7,8},{8,9},{9,10},{10,1... | collective-permute-start | bytes 599048 | tf_op jit(solution)/shard_map/ppermute | solution.py:23
  22.1 12.8 %copy-start.100 = (pred[128]{0:T(512)(128)(4,1)}, pred[128]{0:T(512)(128)(4,1)S(1)}, u32[]{:S(2)}) copy-start(pred[128]{0:T(512)(128)(4,1)S(1)} %get-tuple-element.140) | copy-start | bytes 388
  22.1 12.8 %copy-start.103 = (pred[128]{0:T(512)(128)(4,1)}, pred[128]{0:T(512)(128)(4,1)S(1)}, u32[]{:S(2)}) copy-start(pred[128]{0:T(512)(128)(4,1)S(1)} %get-tuple-element.141) | copy-start | bytes 388
  22.8 12.2 %copy-start.66 = (pred[128]{0:T(512)(128)(4,1)}, pred[128]{0:T(512)(128)(4,1)S(1)}, u32[]{:S(2)}) copy-start(pred[128]{0:T(512)(128)(4,1)S(1)} %get-tuple-element.112) | copy-start | bytes 388
  22.8 12.2 %copy-start.68 = (pred[128]{0:T(512)(128)(4,1)}, pred[128]{0:T(512)(128)(4,1)S(1)}, u32[]{:S(2)}) copy-start(pred[128]{0:T(512)(128)(4,1)S(1)} %get-tuple-element.114) | copy-start | bytes 388
  22.8 12.2 %copy-start.70 = (pred[128]{0:T(512)(128)(4,1)}, pred[128]{0:T(512)(128)(4,1)S(1)}, u32[]{:S(2)}) copy-start(pred[128]{0:T(512)(128)(4,1)S(1)} %get-tuple-element.116) | copy-start | bytes 388
  22.8 12.2 %copy-start.72 = (pred[128]{0:T(512)(128)(4,1)}, pred[128]{0:T(512)(128)(4,1)S(1)}, u32[]{:S(2)}) copy-start(pred[128]{0:T(512)(128)(4,1)S(1)} %get-tuple-element.117) | copy-start | bytes 388
  22.8 12.2 %copy-start.109 = (pred[128]{0:T(512)(128)(4,1)}, pred[128]{0:T(512)(128)(4,1)S(1)}, u32[]{:S(2)}) copy-start(pred[128]{0:T(512)(128)(4,1)S(1)} %get-tuple-element.110) | copy-start | bytes 388
  22.8 12.2 %copy-start.111 = (pred[128]{0:T(512)(128)(4,1)}, pred[128]{0:T(512)(128)(4,1)S(1)}, u32[]{:S(2)}) copy-start(pred[128]{0:T(512)(128)(4,1)S(1)} %get-tuple-element.102) | copy-start | bytes 388
  22.9 12.1 %copy-start.92 = (pred[128]{0:T(512)(128)(4,1)}, pred[128]{0:T(512)(128)(4,1)S(1)}, u32[]{:S(2)}) copy-start(pred[128]{0:T(512)(128)(4,1)S(1)} %get-tuple-element.71) | copy-start | bytes 388
  22.9 12.1 %copy-start.74 = (pred[128]{0:T(512)(128)(4,1)}, pred[128]{0:T(512)(128)(4,1)S(1)}, u32[]{:S(2)}) copy-start(pred[128]{0:T(512)(128)(4,1)S(1)} %get-tuple-element.118) | copy-start | bytes 388
  23.0 12.1 %copy-start.77 = (pred[128]{0:T(512)(128)(4,1)}, pred[128]{0:T(512)(128)(4,1)S(1)}, u32[]{:S(2)}) copy-start(pred[128]{0:T(512)(128)(4,1)S(1)} %get-tuple-element.119) | copy-start | bytes 388
  23.0 12.1 %copy-start.80 = (pred[128]{0:T(512)(128)(4,1)}, pred[128]{0:T(512)(128)(4,1)S(1)}, u32[]{:S(2)}) copy-start(pred[128]{0:T(512)(128)(4,1)S(1)} %get-tuple-element.120) | copy-start | bytes 388
  23.0 12.1 %copy-start.83 = (pred[128]{0:T(512)(128)(4,1)}, pred[128]{0:T(512)(128)(4,1)S(1)}, u32[]{:S(2)}) copy-start(pred[128]{0:T(512)(128)(4,1)S(1)} %get-tuple-element.121) | copy-start | bytes 388
  23.0 12.1 %copy-start.86 = (pred[128]{0:T(512)(128)(4,1)}, pred[128]{0:T(512)(128)(4,1)S(1)}, u32[]{:S(2)}) copy-start(pred[128]{0:T(512)(128)(4,1)S(1)} %get-tuple-element.122) | copy-start | bytes 388
  23.0 12.1 %copy-start.89 = (pred[128]{0:T(512)(128)(4,1)}, pred[128]{0:T(512)(128)(4,1)S(1)}, u32[]{:S(2)}) copy-start(pred[128]{0:T(512)(128)(4,1)S(1)} %get-tuple-element.125) | copy-start | bytes 388
  23.0 12.1 %copy-start.113 = (pred[128]{0:T(512)(128)(4,1)}, pred[128]{0:T(512)(128)(4,1)S(1)}, u32[]{:S(2)}) copy-start(pred[128]{0:T(512)(128)(4,1)S(1)} %get-tuple-element.73) | copy-start | bytes 388
  39.8 50.2 %copy-start.124 = (s32[48]{0:T(128)S(1)}, s32[48]{0:T(128)}, u32[]{:S(2)}) copy-start(s32[48]{0:T(128)} %param.14) | copy-start | bytes 580
  41.0 49.2 %all-to-all-start = ((bf16[128,3,16,96]{0,3,1,2:T(8,128)(2,1)}), bf16[128,3,16,96]{0,3,1,2:T(8,128)(2,1)S(1)}, u32[]{:S(2)}, u32[]{:S(2)}) async-start(bf16[128,3,16,96]{0,3,1,2:T(8,128)(2,1)} %copy.146), calls=%async_computation | async-start | bytes 2359296 | tf_op jit(solution)/shard_map/all_to_all | solution.py:106
  45.0 166.4 %all-gather.7.cloned.1.call-start = ((), (), s32[]{:S(2)}) async-start(), calls=%async_computation.7 | async-start | bytes 5013504 | tf_op jit(solution)/shard_map/all_gather | solution.py:190
  144.5 19.0 %all-to-all-start.2 = ((bf16[128,16,96]{0,2,1:T(8,128)(2,1)}), bf16[128,16,96]{0,2,1:T(8,128)(2,1)S(1)}, u32[]{:S(2)}, u32[]{:S(2)}) async-start(bf16[128,16,96]{0,2,1:T(8,128)(2,1)} %bitcast.34), calls=%async_computation.2 | async-start | bytes 786432 | tf_op jit(solution)/shard_map/all_to_all | solution.py:171
  164.3 38.7 %all-to-all-start.4 = ((bf16[128,16,96]{0,2,1:T(8,128)(2,1)}), bf16[128,16,96]{0,2,1:T(8,128)(2,1)}, u32[]{:S(2)}, u32[]{:S(2)}) async-start(bf16[128,16,96]{0,2,1:T(8,128)(2,1)} %copy.164), calls=%async_computation.4 | async-start | bytes 786432 | tf_op jit(solution)/shard_map/all_to_all | solution.py:178
  203.0 170.2 %all-to-all-start.3 = ((bf16[2048,3,1,96]{3,1,2,0:T(4,128)(2,1)}), bf16[2048,3,1,96]{3,1,2,0:T(4,128)(2,1)}, u32[]{:S(2)}, u32[]{:S(2)}) async-start(bf16[2048,3,1,96]{3,1,2,0:T(4,128)(2,1)} %copy.156), calls=%async_computation.3 | async-start | bytes 4194304 | tf_op jit(solution)/shard_map/all_to_all | solution.py:235
  209.3 162.1 %all-reduce.3.cloned.1.call-start = ((), (), s32[]{:S(2)}) async-start(), calls=%async_computation.6 | async-start | bytes 884736 | tf_op jit(solution)/shard_map/psum | solution.py:193
  379.1 12.7 %copy-start.21 = (bf16[65,1,1536]{0,2,1:T(8,128)(2,1)S(1)}, bf16[65,1,1536]{0,2,1:T(8,128)(2,1)}, u32[]{:S(2)}) copy-start(bf16[65,1,1536]{0,2,1:T(8,128)(2,1)} %get-tuple-element.87) | copy-start | bytes 599044
  380.6 14.7 %copy-start.58 = (f32[1536]{0:T(1024)S(1)}, f32[1536]{0:T(1024)}, u32[]{:S(2)}) copy-start(f32[1536]{0:T(1024)} %get-tuple-element.41) | copy-start | bytes 18436
  384.8 107.9 %collective-permute-start.3 = (bf16[65,1536]{1,0:T(8,128)(2,1)S(1)}, bf16[65,1536]{1,0:T(8,128)(2,1)S(1)}, u32[]{:S(2)}, u32[]{:S(2)}) collective-permute-start(bf16[65,1536]{1,0:T(8,128)(2,1)S(1)} %bitcast.347), channel_id=1, source_target_pairs={{1,0},{2,1},{3,2},{4,3},{5,4},{6,5},{7,6},{8,7},{9,8},{10,9},{11,1... | collective-permute-start | bytes 599048 | tf_op jit(solution)/shard_map/ppermute | solution.py:24
  392.1 100.6 %collective-permute-start.2 = (bf16[65,1536]{1,0:T(8,128)(2,1)S(1)}, bf16[65,1536]{1,0:T(8,128)(2,1)S(1)}, u32[]{:S(2)}, u32[]{:S(2)}) collective-permute-start(bf16[65,1536]{1,0:T(8,128)(2,1)S(1)} %bitcast.348), channel_id=1, source_target_pairs={{0,1},{1,2},{2,3},{3,4},{4,5},{5,6},{6,7},{7,8},{8,9},{9,10},{10,1... | collective-permute-start | bytes 599048 | tf_op jit(solution)/shard_map/ppermute | solution.py:23
  (104 other events, 542.1 us)
Sparse Core Ops, SparseCore 0:
  10.1 62.2 all-gather.4
  74.6 53.0 all-gather.6
  215.9 155.4 all-reduce.2
where the time goes:
time: 524 us; the launch traced here: 518 us
  blocking collectives  160 us (31%)
  waiting for transfers between devices  158 us (30%)
  local copies, waits for them, and re-layouts  67.4 us (13%)
  matrix products  46.9 us (9%)
  starting transfers between devices  40.1 us (8%)
  other arithmetic  28.9 us (6%)
  between operations  16.1 us (3%)
    psum x1, waiting for transfers between devices, local(): weight_sum = lax.psum(weight_local, 'dp') / pack_count  151 us
    psum x1, blocking collectives, local(): gain_sum, taps_sum = lax.psum((pack_gain, taps_grad), ('dp', 'seq'))  96.1 us
    all_gather x1, blocking collectives, local(): rows_all = lax.all_gather(rows_local, 'seq', axis=1, tiled=True)  44.2 us
    gather x18, local copies, waits for them, and re-layouts, neighbour(): jnp.take(padded, source, axis=0)  23.2 us
    all_to_all x1, blocking collectives, local(): lax.all_to_all(attention_heads, 'seq', split_axis=0, concat_axis=1, tiled...  19.7 us
    ppermute x2, starting transfers between devices, with_halo(): after = lax.ppermute(initial, axis, down)  15.8 us
    unnamed x258, local copies, waits for them, and re-layouts  12.1 us
  transfers between devices with their start and end apart: 11, of which 2 were waited for; matrix products, arithmetic and copies ran while one was open for 22% of the time, Pallas kernels for 0%

commit v1 on v0

--- a/solution.py
+++ b/solution.py
@@ -11,6 +11,10 @@
 feature_floor = 0.1
 epsilon = 1e-06
 highest = lax.Precision.HIGHEST
+
+
+def prepare_the_lots_all(message):
+    return jnp.sum(jax.lax.all_gather(message, "dp"), axis=0)
 
 
 def with_halo(shard, sides, width):
@@ -190,7 +194,7 @@
         lax.all_gather(grad_in, "seq", axis=0, tiled=True),
         preferred_element_type=jnp.float32,
     )
-    weight_sum = lax.psum(weight_local, "dp") / pack_count
+    weight_sum = prepare_the_lots_all(weight_local) / pack_count
     grad_float = heads_last(grad_arrived.reshape(all_rows, local_width), head_count).astype(
         jnp.float32
     )

time: 524 us -> 437 us (0.83)
  waiting for transfers between devices: 158 us -> 65.9 us
  other arithmetic: 28.9 us -> 35.1 us
  starting transfers between devices: 40.1 us -> 34.7 us
    psum x1 -> x0, waiting for transfers between devices: 151 us -> none  [local(): weight_sum = lax.psum(weight_local, 'dp') / pack_count]
    all_to_all x1, waiting for transfers between devices: 0.01 us -> 42.8 us  [local(): lax.all_to_all(jnp.stack([grad_queries, grad_keys, grad_conv], axis=1).re...]
    all_to_all x1, waiting for transfers between devices: 0.01 us -> 12.9 us  [local(): lax.all_to_all(attention_heads, 'seq', split_axis=0, concat_axis=1, tiled...]
    reduce_sum x0 -> x1, other arithmetic: none -> 5.69 us  [prepare_the_lots_all(): return jnp.sum(jax.lax.all_gather(message, 'dp'), axis=0)]
    unnamed x258 -> x264, local copies, waits for them, and re-layouts: 12.1 us -> 14.3 us
  transfers between devices with their start and end apart: 11 -> 11, of which waited for: 2 -> 3; matrix products, arithmetic and copies ran while one was open for 22% -> 33% of each run, Pallas kernels for 0% -> 0%
where the time goes in v1:
time: 437 us; the launch traced here: 430 us
  blocking collectives  165 us (38%)
  local copies, waits for them, and re-layouts  70.1 us (16%)
  waiting for transfers between devices  65.9 us (15%)
  matrix products  43.5 us (10%)
  other arithmetic  35.1 us (8%)
  starting transfers between devices  34.7 us (8%)
  between operations  16.1 us (4%)
    psum x1, blocking collectives, local(): gain_sum, taps_sum = lax.psum((pack_gain, taps_grad), ('dp', 'seq'))  99.6 us
    all_gather x1, blocking collectives, local(): rows_all = lax.all_gather(rows_local, 'seq', axis=1, tiled=True)  46.6 us
    all_to_all x1, waiting for transfers between devices, local(): lax.all_to_all(jnp.stack([grad_queries, grad_keys, grad_conv], axis=1).re...  42.8 us
    gather x18, local copies, waits for them, and re-layouts, neighbour(): jnp.take(padded, source, axis=0)  23.3 us
    all_to_all x1, blocking collectives, local(): lax.all_to_all(normed.reshape(tok_rows, groups, local_width), 'seq', spli...  18.8 us
    unnamed x264, local copies, waits for them, and re-layouts  14.3 us
    all_to_all x1, waiting for transfers between devices, local(): lax.all_to_all(attention_heads, 'seq', split_axis=0, concat_axis=1, tiled...  12.9 us
    ppermute x2, starting transfers between devices, with_halo(): after = lax.ppermute(initial, axis, down)  11.3 us
  transfers between devices with their start and end apart: 11, of which 3 were waited for; matrix products, arithmetic and copies ran while one was open for 33% of the time, Pallas kernels for 0%

profile of v1, /device:TPU:1, one launch (start us, length us, event | category | flops | bytes accessed | tf_op | source)
XLA Modules:
  0.0 430.3 jit_solution(10221225819187990218)
XLA Ops:
  9.0 8.8 %collective-permute-start.1 = (bf16[65,1536]{1,0:T(8,128)(2,1)S(1)}, bf16[65,1536]{1,0:T(8,128)(2,1)S(1)}, u32[]{:S(2)}, u32[]{:S(2)}) collective-permute-start(bf16[65,1536]{1,0:T(8,128)(2,1)S(1)} %get-tuple-element.93), channel_id=1, source_target_pairs={{1,0},{2,1},{3,2},{4,3},{5,4},{6,5},{7,6},{8,7},{9,8},{10,9},{11,1... | collective-permute-start | bytes 599048 | tf_op jit(solution)/shard_map/ppermute | solution.py:28
  35.3 3.3 fusion.69
  41.1 4.0 all-to-all-start
  46.0 46.6 %all-gather = s32[1,5,2048]{2,0,1:T(1,128)S(1)} all-gather(s32[1,5,128]{2,0,1:T(1,128)S(1)} %copy-done.59), channel_id=2, replica_groups=mesh['dp'=32,'seq'=16] {'seq'}, dimensions={2}, use_global_device_ids=true | all-gather | bytes 43520 | tf_op jit(solution)/shard_map/all_gather | solution.py:106
  93.8 2.5 fusion.32
  97.2 4.0 add_convert_fusion
  108.7 2.6 reshape.593
  111.3 5.3 %all-to-all-start.1 = ((bf16[16,2,6144]{2,1,0:T(2,128)(2,1)}), bf16[16,2,6144]{2,1,0:T(2,128)(2,1)S(1)}, u32[]{:S(2)}, u32[]{:S(2)}) async-start(bf16[16,2,6144]{2,1,0:T(2,128)(2,1)} %reshape.593), calls=%async_computation.1 | async-start | bytes 786432 | tf_op jit(solution)/shard_map/all_to_all | solution.py:159
  118.8 12.9 %all-to-all-done.1 = bf16[16,2,6144]{2,1,0:T(2,128)(2,1)S(1)} async-done(((bf16[16,2,6144]{2,1,0:T(2,128)(2,1)}), bf16[16,2,6144]{2,1,0:T(2,128)(2,1)S(1)}, u32[]{:S(2)}, u32[]{:S(2)}) %all-to-all-start.1) | async-done | bytes 393248 | tf_op jit(solution)/shard_map/all_to_all | solution.py:159
  133.6 2.3 copy.149
  137.4 18.8 %all_to_all.63 = bf16[128,16,96]{0,2,1:T(8,128)(2,1)S(1)} all-to-all(bf16[128,16,96]{0,2,1:T(8,128)(2,1)S(1)} %copy.164), channel_id=1, replica_groups=mesh['dp'=32,'seq'=16] {'seq'}, dimensions={1} | all-to-all | bytes 786432 | tf_op jit(solution)/shard_map/all_to_all | solution.py:182
  156.4 4.0 fusion.4
  160.4 2.3 copy.150
  165.0 4.2 multiply_reduce_fusion
  171.1 4.3 all-to-all-start.2
  175.4 5.0 %fusion.31 = u8[256,2048]{1,0:T(8,128)(4,1)} fusion(f32[3,256,2048]{2,1,0:T(8,128)} %get-tuple-element.128), kind=kLoop, calls=%fused_computation.63 | loop fusion | flops 8912896 | bytes 6815744
  180.4 8.8 %all-to-all-done.2 = bf16[128,16,96]{0,2,1:T(8,128)(2,1)} async-done(((bf16[128,16,96]{0,2,1:T(8,128)(2,1)}), bf16[128,16,96]{0,2,1:T(8,128)(2,1)}, u32[]{:S(2)}, u32[]{:S(2)}) %all-to-all-start.2) | async-done | bytes 393248 | tf_op jit(solution)/shard_map/all_to_all | solution.py:175
  195.4 2.5 convolution_convert_fusion.1
  199.1 3.7 fusion.121
  202.8 4.6 %fusion.107 = f32[3,256,2048]{2,1,0:T(8,128)} fusion(bf16[3,3,256]{2,1,0:T(4,128)(2,1)S(1)} %copy-done.56, f32[3,2048]{1,0:T(4,128)S(1)} %multiply_divide_fusion, f32[3,2048]{1,0:T(4,128)S(1)} %copy-done.19), kind=kOutput, calls=%fused_computation.167 | convolution fusion | flops 56641536 | bytes 6345216 | tf_op jit(solution)/shard_map/hit,hif->hft/dot_general | solution.py:212
  208.8 4.8 %fusion.21 = bf16[3,32,2048]{2,1,0:T(8,128)(2,1)S(1)} fusion(f32[3,256,2048]{2,1,0:T(8,128)} %fusion.121, bf16[3,3,256,32]{2,3,1,0:T(8,128)(2,1)S(1)} %fusion.54, u8[256,2048]{1,0:T(8,128)(4,1)S(1)} %copy-done.25, bf16[3,32,2048]{2,1,0:T(8,128)(2,1)S(1)} %bitcast.349, bf16[3,2048]{1,0:T(4,128)(2,1)S(1)} %copy-done.61, s32[32,256]{1,0:T(8,128)S(1)} %copy-done.32, ...), kind=kOutput, calls=%fused_computation.56 | convolution fusion | flops 415113216 | bytes 7794700 | tf_op jit(solution)/shard_map/hft,hef->het/dot_general | solution.py:228
  213.6 4.9 %fusion.20 = bf16[3,32,2048]{2,1,0:T(8,128)(2,1)S(1)} fusion(f32[3,256,2048]{2,1,0:T(8,128)} %fusion.107, bf16[3,3,256,32]{2,3,1,0:T(8,128)(2,1)S(1)} %copy-done.35, u8[256,2048]{1,0:T(8,128)(4,1)S(1)} %copy-done.26, bf16[3,32,2048]{2,1,0:T(8,128)(2,1)S(1)} %copy-done.30, bf16[3,2048]{1,0:T(4,128)(2,1)S(1)} %copy-done.61, s32[32,256]{1,0:T(8,128)S(1)} %copy-done.32, ...), kind=kOutput, calls=%fused_computation.55 | convolution fusion | flops 415113216 | bytes 7794700 | tf_op jit(solution)/shard_map/hft,hef->het/dot_general | solution.py:217
  219.7 4.2 copy.156
  224.0 4.6 %all-to-all-start.3 = ((bf16[2048,3,1,96]{3,1,2,0:T(4,128)(2,1)}), bf16[2048,3,1,96]{3,1,2,0:T(4,128)(2,1)}, u32[]{:S(2)}, u32[]{:S(2)}) async-start(bf16[2048,3,1,96]{3,1,2,0:T(4,128)(2,1)} %copy.156), calls=%async_computation.3 | async-start | bytes 4194304 | tf_op jit(solution)/shard_map/all_to_all | solution.py:239
  231.0 2.6 fusion.22
  233.6 42.8 %all-to-all-done.3 = bf16[2048,3,1,96]{3,1,2,0:T(4,128)(2,1)} async-done(((bf16[2048,3,1,96]{3,1,2,0:T(4,128)(2,1)}), bf16[2048,3,1,96]{3,1,2,0:T(4,128)(2,1)}, u32[]{:S(2)}, u32[]{:S(2)}) %all-to-all-start.3) | async-done | bytes 1179680 | tf_op jit(solution)/shard_map/all_to_all | solution.py:239
  276.4 3.0 copy.173
  284.3 2.5 collective-permute-start.3
  289.9 3.2 collective-permute-start.2
  297.3 99.6 %all-reduce = (f32[1536]{0:T(1024)S(1)}, f32[9,1536]{1,0:T(8,128)S(1)}) all-reduce(f32[1536]{0:T(1024)S(1)} %copy-done.57, f32[9,1536]{1,0:T(8,128)S(1)} %stack.64), channel_id=1, replica_groups=mesh['dp'=32,'seq'=16] {'dp','seq'}, use_global_device_ids=true, to_apply=%region_9.11 | all-reduce | flops 15360 | bytes 122880 | tf_op jit(solution)/shard_map/psum | solution.py:254
  412.5 2.8 fusion.103
  417.1 5.7 %reduce_sum.171 = f32[96,1152]{1,0:T(8,128)S(1)} reduce(f32[32,96,1152]{2,1,0:T(8,128)} %bitcast.328, f32[]{:T(128)} %constant.82.clone.1), dimensions={0}, to_apply=%region_7.9 | reduce | flops 3428352 | bytes 14598148 | tf_op jit(solution)/shard_map/reduce_sum | solution.py:17
  (379 shorter events, 83.0 us)
Async XLA Ops:
  7.2 14.9 %copy-start.59 = (s32[1,5,128]{2,0,1:T(1,128)S(1)}, s32[1,5,128]{2,0,1:T(1,128)}, u32[]{:S(2)}) copy-start(s32[1,5,128]{2,0,1:T(1,128)} %param.15) | copy-start | bytes 7684
  7.2 16.9 %copy-start.58 = (f32[9,1536]{1,0:T(8,128)S(1)}, f32[9,1536]{1,0:T(8,128)}, u32[]{:S(2)}) copy-start(f32[9,1536]{1,0:T(8,128)} %param.13) | copy-start | bytes 165892
  7.2 149.2 %all-gather.9.cloned.1.call-start = ((), (), s32[]{:S(2)}) async-start(), calls=%async_computation.6 | async-start | bytes 5013504 | tf_op jit(solution)/shard_map/all_gather | solution.py:194
  9.0 15.4 %collective-permute-start.1 = (bf16[65,1536]{1,0:T(8,128)(2,1)S(1)}, bf16[65,1536]{1,0:T(8,128)(2,1)S(1)}, u32[]{:S(2)}, u32[]{:S(2)}) collective-permute-start(bf16[65,1536]{1,0:T(8,128)(2,1)S(1)} %get-tuple-element.93), channel_id=1, source_target_pairs={{1,0},{2,1},{3,2},{4,3},{5,4},{6,5},{7,6},{8,7},{9,8},{10,9},{11,1... | collective-permute-start | bytes 599048 | tf_op jit(solution)/shard_map/ppermute | solution.py:28
  17.8 6.6 %collective-permute-start = (bf16[65,1536]{1,0:T(8,128)(2,1)S(1)}, bf16[65,1536]{1,0:T(8,128)(2,1)S(1)}, u32[]{:S(2)}, u32[]{:S(2)}) collective-permute-start(bf16[65,1536]{1,0:T(8,128)(2,1)S(1)} %get-tuple-element.92), channel_id=1, source_target_pairs={{0,1},{1,2},{2,3},{3,4},{4,5},{5,6},{6,7},{7,8},{8,9},{9,10},{10,1... | collective-permute-start | bytes 599048 | tf_op jit(solution)/shard_map/ppermute | solution.py:27
  41.1 51.5 %all-to-all-start = ((bf16[128,3,16,96]{0,3,1,2:T(8,128)(2,1)}), bf16[128,3,16,96]{0,3,1,2:T(8,128)(2,1)S(1)}, u32[]{:S(2)}, u32[]{:S(2)}) async-start(bf16[128,3,16,96]{0,3,1,2:T(8,128)(2,1)} %copy.146), calls=%async_computation | async-start | bytes 2359296 | tf_op jit(solution)/shard_map/all_to_all | solution.py:110
  45.1 119.9 %all-gather.7.cloned.1.call-start = ((), (), s32[]{:S(2)}) async-start(), calls=%async_computation.5 | async-start | bytes 3760128 | tf_op jit(solution)/shard_map/all_gather | solution.py:165
  46.0 51.2 %copy-start.116 = (s32[3]{0:T(128)}, s32[3]{0:T(128)S(1)}, u32[]{:S(2)}) copy-start(s32[3]{0:T(128)S(1)} %dynamic-slice_multiply_fusion) | copy-start | bytes 40
  111.3 20.3 %all-to-all-start.1 = ((bf16[16,2,6144]{2,1,0:T(2,128)(2,1)}), bf16[16,2,6144]{2,1,0:T(2,128)(2,1)S(1)}, u32[]{:S(2)}, u32[]{:S(2)}) async-start(bf16[16,2,6144]{2,1,0:T(2,128)(2,1)} %reshape.593), calls=%async_computation.1 | async-start | bytes 786432 | tf_op jit(solution)/shard_map/all_to_all | solution.py:159
  116.7 300.4 %all-gather.11.cloned.1.call-start = ((), (), s32[]{:S(2)}) async-start(), calls=%async_computation.7 | async-start | bytes 14598144 | tf_op jit(solution)/shard_map/all_gather | solution.py:17
  137.0 19.1 %copy-start.62 = (f32[128]{0:T(128)}, f32[128]{0:T(128)S(1)}, u32[]{:S(2)}) copy-start(f32[128]{0:T(128)S(1)} %add_rsqrt_fusion) | copy-start | bytes 1540
  171.1 18.1 %all-to-all-start.2 = ((bf16[128,16,96]{0,2,1:T(8,128)(2,1)}), bf16[128,16,96]{0,2,1:T(8,128)(2,1)}, u32[]{:S(2)}, u32[]{:S(2)}) async-start(bf16[128,16,96]{0,2,1:T(8,128)(2,1)} %bitcast.34), calls=%async_computation.2 | async-start | bytes 786432 | tf_op jit(solution)/shard_map/all_to_all | solution.py:175
  180.4 15.0 %copy-start.19 = (f32[3,2048]{1,0:T(4,128)S(1)}, f32[3,2048]{1,0:T(4,128)}, u32[]{:S(2)}) copy-start(f32[3,2048]{1,0:T(4,128)} %copy-done.18) | copy-start | bytes 73732
  224.0 52.5 %all-to-all-start.3 = ((bf16[2048,3,1,96]{3,1,2,0:T(4,128)(2,1)}), bf16[2048,3,1,96]{3,1,2,0:T(4,128)(2,1)}, u32[]{:S(2)}, u32[]{:S(2)}) async-start(bf16[2048,3,1,96]{3,1,2,0:T(4,128)(2,1)} %copy.156), calls=%async_computation.3 | async-start | bytes 4194304 | tf_op jit(solution)/shard_map/all_to_all | solution.py:239
  279.4 13.7 %copy-start.6 = (bf16[128,1536]{1,0:T(8,128)(2,1)S(1)}, bf16[128,1536]{1,0:T(8,128)(2,1)}, u32[]{:S(2)}) copy-start(bf16[128,1536]{1,0:T(8,128)(2,1)} %copy-done.5) | copy-start | bytes 1179652
  279.4 13.7 %copy-start.8 = (bf16[128,1536]{1,0:T(8,128)(2,1)S(1)}, bf16[128,1536]{1,0:T(8,128)(2,1)}, u32[]{:S(2)}) copy-start(bf16[128,1536]{1,0:T(8,128)(2,1)} %copy-done.7) | copy-start | bytes 1179652
  279.4 13.7 %copy-start.10 = (bf16[128,1536]{1,0:T(8,128)(2,1)S(1)}, bf16[128,1536]{1,0:T(8,128)(2,1)}, u32[]{:S(2)}) copy-start(bf16[128,1536]{1,0:T(8,128)(2,1)} %copy-done.9) | copy-start | bytes 1179652
  279.4 13.7 %copy-start.12 = (bf16[128,1536]{1,0:T(8,128)(2,1)S(1)}, bf16[128,1536]{1,0:T(8,128)(2,1)}, u32[]{:S(2)}) copy-start(bf16[128,1536]{1,0:T(8,128)(2,1)} %copy-done.11) | copy-start | bytes 1179652
  279.4 13.7 %copy-start.14 = (bf16[128,1536]{1,0:T(8,128)(2,1)S(1)}, bf16[128,1536]{1,0:T(8,128)(2,1)}, u32[]{:S(2)}) copy-start(bf16[128,1536]{1,0:T(8,128)(2,1)} %copy-done.13) | copy-start | bytes 1179652
  279.4 13.7 %copy-start.72 = (pred[128]{0:T(512)(128)(4,1)S(1)}, pred[128]{0:T(512)(128)(4,1)}, u32[]{:S(2)}) copy-start(pred[128]{0:T(512)(128)(4,1)} %copy-done.71) | copy-start | bytes 388
  279.5 13.7 %copy-start.74 = (pred[128]{0:T(512)(128)(4,1)S(1)}, pred[128]{0:T(512)(128)(4,1)}, u32[]{:S(2)}) copy-start(pred[128]{0:T(512)(128)(4,1)} %copy-done.73) | copy-start | bytes 388
  279.5 13.7 %copy-start.80 = (pred[128]{0:T(512)(128)(4,1)S(1)}, pred[128]{0:T(512)(128)(4,1)}, u32[]{:S(2)}) copy-start(pred[128]{0:T(512)(128)(4,1)} %copy-done.79) | copy-start | bytes 388
  279.5 13.7 %copy-start.83 = (pred[128]{0:T(512)(128)(4,1)S(1)}, pred[128]{0:T(512)(128)(4,1)}, u32[]{:S(2)}) copy-start(pred[128]{0:T(512)(128)(4,1)} %copy-done.82) | copy-start | bytes 388
  279.5 13.7 %copy-start.86 = (pred[128]{0:T(512)(128)(4,1)S(1)}, pred[128]{0:T(512)(128)(4,1)}, u32[]{:S(2)}) copy-start(pred[128]{0:T(512)(128)(4,1)} %copy-done.85) | copy-start | bytes 388
  281.3 14.2 %copy-start.66 = (pred[128]{0:T(512)(128)(4,1)S(1)}, pred[128]{0:T(512)(128)(4,1)}, u32[]{:S(2)}) copy-start(pred[128]{0:T(512)(128)(4,1)} %copy-done.65) | copy-start | bytes 388
  281.3 14.2 %copy-start.68 = (pred[128]{0:T(512)(128)(4,1)S(1)}, pred[128]{0:T(512)(128)(4,1)}, u32[]{:S(2)}) copy-start(pred[128]{0:T(512)(128)(4,1)} %copy-done.67) | copy-start | bytes 388
  281.3 14.2 %copy-start.70 = (pred[128]{0:T(512)(128)(4,1)S(1)}, pred[128]{0:T(512)(128)(4,1)}, u32[]{:S(2)}) copy-start(pred[128]{0:T(512)(128)(4,1)} %copy-done.69) | copy-start | bytes 388
  281.3 14.2 %copy-start.77 = (pred[128]{0:T(512)(128)(4,1)S(1)}, pred[128]{0:T(512)(128)(4,1)}, u32[]{:S(2)}) copy-start(pred[128]{0:T(512)(128)(4,1)} %copy-done.76) | copy-start | bytes 388
  281.3 14.2 %copy-start.106 = (pred[128]{0:T(512)(128)(4,1)S(1)}, pred[128]{0:T(512)(128)(4,1)}, u32[]{:S(2)}) copy-start(pred[128]{0:T(512)(128)(4,1)} %copy-done.105) | copy-start | bytes 388
  281.3 14.2 %copy-start.109 = (pred[128]{0:T(512)(128)(4,1)S(1)}, pred[128]{0:T(512)(128)(4,1)}, u32[]{:S(2)}) copy-start(pred[128]{0:T(512)(128)(4,1)} %copy-done.108) | copy-start | bytes 388
  284.3 113.7 %collective-permute-start.3 = (bf16[65,1536]{1,0:T(8,128)(2,1)}, bf16[65,1536]{1,0:T(8,128)(2,1)S(1)}, u32[]{:S(2)}, u32[]{:S(2)}) collective-permute-start(bf16[65,1536]{1,0:T(8,128)(2,1)} %bitcast.60), channel_id=1, source_target_pairs={{1,0},{2,1},{3,2},{4,3},{5,4},{6,5},{7,6},{8,7},{9,8},{10,9},{11,1... | collective-permute-start | bytes 599048 | tf_op jit(solution)/shard_map/ppermute | solution.py:28
  289.9 108.2 %collective-permute-start.2 = (bf16[65,1536]{1,0:T(8,128)(2,1)}, bf16[65,1536]{1,0:T(8,128)(2,1)}, u32[]{:S(2)}, u32[]{:S(2)}) collective-permute-start(bf16[65,1536]{1,0:T(8,128)(2,1)} %bitcast.352), channel_id=1, source_target_pairs={{0,1},{1,2},{2,3},{3,4},{4,5},{5,6},{6,7},{7,8},{8,9},{9,10},{10,1... | collective-permute-start | bytes 599048 | tf_op jit(solution)/shard_map/ppermute | solution.py:27
  (107 other events, 797.8 us)
Sparse Core Ops, SparseCore 0:
  10.1 73.7 all-gather.8
  86.0 46.8 all-gather.6
  160.5 130.1 all-gather.10
